TPU v7x, 256 devices: a whole 4x4x8 slice. The times are simulated.
256 devices in a mesh: slab: 64 (over z, x, core), energy: 4 (over y).
Axes of the slice: x: 4, y: 4, z: 8, core: 2. Of those that a mesh axis runs over, the one named last changes fastest.
Arguments:
- energy_sq: float32 [4], P('energy'), may hold values from 2.5 to 3.3
- broadening: float32 [4], P('energy'), may hold values from 0.05 to 0.1
- onsite: float32 [64, 192, 192], P('slab'), may hold values from -0.005051815 to 2
- coupling: float32 [64, 192, 192], P('slab'), may hold values from -0.005051815 to 0.005051815
- sigma_in: float32 [4, 64, 192, 384], P('energy', 'slab'), may hold values from -0.02 to 0.005051815
- anharmonic: float32 [64, 192, 192], P('slab'), may hold values from 0.5 to 2
- energy_pairs: int32 [4, 8, 2], P('energy'), may hold values from 0 to 3
Outputs:
- green_diag: float32 [4, 64, 192, 384], P('energy', 'slab')
- sigma_out: float32 [4, 64, 192, 384], P('energy', 'slab')
All inputs are finite; a program needn't handle non-finite values.
Results may differ from a plain program's by a relative error of at most 0.0003.
Values sent between devices are 32-bit elements; how exact they have to be, the bound alone decides.
A program may use at most 128 MiB of HBM per device.

v0:
```python
import jax
import jax.numpy as jnp
from jax import lax
from jax.sharding import PartitionSpec as P


def shifted(value, axis, steps):
    count = lax.axis_size(axis)
    first, last = (max(0, -steps), min(count, count - steps))
    return lax.ppermute(value, axis, [(source, source + steps) for source in range(first, last)])


def complex_product(left, right):
    block_width = left.shape[-2]
    high = lax.Precision.HIGHEST
    right_real = right[..., :block_width]
    right_imag = right[..., block_width:]
    stacked = jnp.concatenate(
        [
            jnp.concatenate([right_real, right_imag], -1),
            jnp.concatenate([-right_imag, right_real], -1),
        ],
        -2,
    )
    return jnp.einsum("...ij,...jk->...ik", left, stacked, precision=high)


def invert(matrix):
    block_width = matrix.shape[-2]
    high = lax.Precision.HIGHEST
    real_part = matrix[..., :block_width]
    imag_part = matrix[..., block_width:]
    real_part = 0.5 * (real_part + jnp.swapaxes(real_part, -1, -2))
    imag_part = 0.5 * (imag_part + jnp.swapaxes(imag_part, -1, -2))
    identity = jnp.broadcast_to(jnp.eye(block_width, dtype=jnp.float32), real_part.shape)
    imag_factor = jnp.linalg.cholesky(imag_part)
    factor_inverse = jax.scipy.linalg.solve_triangular(imag_factor, identity, lower=True)
    factor_trans = jnp.swapaxes(factor_inverse, -1, -2)
    middle = jnp.einsum(
        "...ij,...jk,...kl->...il", factor_inverse, real_part, factor_trans, precision=high
    )
    middle = 0.5 * (middle + jnp.swapaxes(middle, -1, -2))
    squared = jnp.einsum("...ij,...jk->...ik", middle, middle, precision=high) + identity
    square_factor = jnp.linalg.cholesky(squared)
    right_side = jax.scipy.linalg.cho_solve((square_factor, True), factor_inverse)
    first_real = jnp.einsum(
        "...ij,...jk,...kl->...il", factor_trans, middle, right_side, precision=high
    )
    first_imag = -jnp.einsum("...ij,...jk->...ik", factor_trans, right_side, precision=high)
    first = jnp.concatenate([first_real, first_imag], -1)
    first = 2.0 * first - complex_product(first, complex_product(matrix, first))
    return first


def reduce_levels(matrix, lower_block, upper_block):
    slab_count = lax.axis_size("slab")
    level_count = slab_count.bit_length() - 1
    for level_index in range(level_count):
        distance = 2**level_index
        inverse = invert(matrix)
        forward = complex_product(inverse, upper_block)
        backward = complex_product(inverse, lower_block)
        if level_index + 1 < level_count:
            payload = jnp.stack([forward, backward])
            low_side = shifted(payload, "slab", distance)
            high_side = shifted(payload, "slab", -distance)
            matrix = (
                matrix
                - complex_product(lower_block, low_side[0])
                - complex_product(upper_block, high_side[1])
            )
            new_lower = -complex_product(lower_block, low_side[1])
            new_upper = -complex_product(upper_block, high_side[0])
            lower_block = new_lower
            upper_block = new_upper
        else:
            last_payload = jnp.stack([forward, backward])
            low_pair = shifted(last_payload, "slab", distance)
            high_pair = shifted(last_payload, "slab", -distance)
            low_forward = low_pair[0]
            high_backward = high_pair[1]
            matrix = (
                matrix
                - complex_product(lower_block, low_forward)
                - complex_product(upper_block, high_backward)
            )
    return invert(matrix)


def shards(energy_sq, broadening, onsite, coupling, sigma_in, anharmonic, energy_pairs):
    block_width = onsite.shape[-1]
    energy_count = energy_sq.shape[0]
    identity = jnp.eye(block_width, dtype=jnp.float32)
    blank = jnp.zeros((block_width, block_width), jnp.float32)
    bond_block = identity + coupling[0]
    bond_below = shifted(bond_block, "slab", 1)
    upper_one = jnp.concatenate([-bond_block, blank], -1)
    lower_one = jnp.concatenate([-bond_below.T, blank], -1)
    self_part = sigma_in[:, 0]
    diag_real = (
        energy_sq[:, None, None] * identity[None] - onsite[0][None] - self_part[..., :block_width]
    )
    diag_imag = broadening[:, None, None] * identity[None] - self_part[..., block_width:]
    matrix = jnp.concatenate([diag_real, diag_imag], -1)
    upper_all = jnp.broadcast_to(upper_one, (energy_count, block_width, 2 * block_width))
    lower_all = jnp.broadcast_to(lower_one, (energy_count, block_width, 2 * block_width))
    green_local = reduce_levels(matrix, lower_all, upper_all)
    everyone = lax.all_gather(green_local[:, None], "energy", axis=0, tiled=True)[:, 0]
    pair_count = energy_pairs.shape[1]
    first = jnp.take(everyone, energy_pairs[:, :, 0], axis=0)
    second = jnp.take(everyone, energy_pairs[:, :, 1], axis=0)
    real_part = (
        first[..., :block_width] * second[..., :block_width]
        - first[..., block_width:] * second[..., block_width:]
    )
    imag_part = (
        first[..., :block_width] * second[..., block_width:]
        + first[..., block_width:] * second[..., :block_width]
    )
    summed_real = jnp.sum(real_part, axis=1)
    summed_imag = jnp.sum(imag_part, axis=1)
    scale = anharmonic[0] / pair_count
    sigma_local = jnp.concatenate([summed_real * scale[None], summed_imag * scale[None]], -1)
    return (green_local[:, None], sigma_local[:, None])


def solution(mesh):
    in_specs = (
        P("energy"),
        P("energy"),
        P("slab", None, None),
        P("slab", None, None),
        P("energy", "slab", None, None),
        P("slab", None, None),
        P("energy", None, None),
    )
    out_specs = (P("energy", "slab", None, None), P("energy", "slab", None, None))
    return jax.shard_map(shards, mesh=mesh, in_specs=in_specs, out_specs=out_specs, check_vma=False)
```

profile of v0, /device:TPU:2, one launch (start us, length us, event | category | flops | bytes accessed | tf_op | source)
XLA Modules:
  0.0 1013.1 jit_solution(17196710646150836668)
XLA Ops:
  13.4 11.7 %custom-call.81 = f32[1,128,128]{2,1,0:T(8,128)S(1)} custom-call(f32[1,128,128]{2,1,0:T(8,128)S(1)} %copy.15), custom_call_target="Cholesky" | custom-call | tf_op jit(solution)/shard_map/jit(cholesky)/cholesky | solution.py:36
  44.1 19.9 %custom-call.84 = f32[2,128,128]{1,2,0:T(8,128)S(1)} custom-call(f32[2,128,128]{2,1,0:T(8,128)S(1)} %pad_maximum_fusion.34), custom_call_target="InvertDiagBlocksLowerTriangular" | custom-call | tf_op jit(solution)/shard_map/jit(_solve_triangular)/triangular_solve/custom-call.1 | solution.py:37
  66.9 11.7 %custom-call.85 = f32[1,128,128]{2,1,0:T(8,128)S(1)} custom-call(f32[1,128,128]{2,1,0:T(8,128)S(1)} %cholesky.1192), custom_call_target="Cholesky" | custom-call | tf_op jit(solution)/shard_map/jit(cholesky)/cholesky | solution.py:44
  97.5 20.1 %custom-call.88 = f32[2,128,128]{1,2,0:T(8,128)S(1)} custom-call(f32[2,128,128]{2,1,0:T(8,128)S(1)} %pad_maximum_fusion.35), custom_call_target="InvertDiagBlocksLowerTriangular" | custom-call | tf_op jit(solution)/shard_map/jit(_cho_solve)/triangular_solve | solution.py:45
  141.4 11.7 %custom-call.90 = f32[1,128,128]{2,1,0:T(8,128)S(1)} custom-call(f32[1,128,128]{2,1,0:T(8,128)S(1)} %copy.29), custom_call_target="Cholesky" | custom-call | tf_op jit(solution)/shard_map/jit(cholesky)/cholesky | solution.py:36
  172.3 19.9 %custom-call.93 = f32[2,128,128]{1,2,0:T(8,128)S(1)} custom-call(f32[2,128,128]{2,1,0:T(8,128)S(1)} %pad_maximum_fusion.36), custom_call_target="InvertDiagBlocksLowerTriangular" | custom-call | tf_op jit(solution)/shard_map/jit(_solve_triangular)/triangular_solve/custom-call.1 | solution.py:37
  195.1 11.7 %custom-call.94 = f32[1,128,128]{2,1,0:T(8,128)S(1)} custom-call(f32[1,128,128]{2,1,0:T(8,128)S(1)} %cholesky.1198), custom_call_target="Cholesky" | custom-call | tf_op jit(solution)/shard_map/jit(cholesky)/cholesky | solution.py:44
  225.7 20.1 %custom-call.97 = f32[2,128,128]{1,2,0:T(8,128)S(1)} custom-call(f32[2,128,128]{2,1,0:T(8,128)S(1)} %pad_maximum_fusion.37), custom_call_target="InvertDiagBlocksLowerTriangular" | custom-call | tf_op jit(solution)/shard_map/jit(_cho_solve)/triangular_solve | solution.py:45
  274.9 11.7 %custom-call.99 = f32[1,128,128]{2,1,0:T(8,128)S(1)} custom-call(f32[1,128,128]{2,1,0:T(8,128)S(1)} %copy.43), custom_call_target="Cholesky" | custom-call | tf_op jit(solution)/shard_map/jit(cholesky)/cholesky | solution.py:36
  305.8 19.9 %custom-call.102 = f32[2,128,128]{1,2,0:T(8,128)S(1)} custom-call(f32[2,128,128]{2,1,0:T(8,128)S(1)} %pad_maximum_fusion.38), custom_call_target="InvertDiagBlocksLowerTriangular" | custom-call | tf_op jit(solution)/shard_map/jit(_solve_triangular)/triangular_solve/custom-call.1 | solution.py:37
  328.5 11.7 %custom-call.103 = f32[1,128,128]{2,1,0:T(8,128)S(1)} custom-call(f32[1,128,128]{2,1,0:T(8,128)S(1)} %cholesky.1204), custom_call_target="Cholesky" | custom-call | tf_op jit(solution)/shard_map/jit(cholesky)/cholesky | solution.py:44
  359.1 20.1 %custom-call.106 = f32[2,128,128]{1,2,0:T(8,128)S(1)} custom-call(f32[2,128,128]{2,1,0:T(8,128)S(1)} %pad_maximum_fusion.39), custom_call_target="InvertDiagBlocksLowerTriangular" | custom-call | tf_op jit(solution)/shard_map/jit(_cho_solve)/triangular_solve | solution.py:45
  407.3 12.6 %collective-permute-done.5 = f32[2,1,192,384]{3,2,1,0:T(8,128)S(1)} collective-permute-done((f32[2,1,192,384]{3,2,1,0:T(8,128)S(1)}, f32[2,1,192,384]{3,2,1,0:T(8,128)S(1)}, u32[]{:S(2)}, u32[]{:S(2)}) %collective-permute-start.5) | collective-permute-done | bytes 589856 | tf_op jit(solution)/shard_map/ppermute | solution.py:10
  422.3 11.7 %custom-call.108 = f32[1,128,128]{2,1,0:T(8,128)S(1)} custom-call(f32[1,128,128]{2,1,0:T(8,128)S(1)} %copy.57), custom_call_target="Cholesky" | custom-call | tf_op jit(solution)/shard_map/jit(cholesky)/cholesky | solution.py:36
  453.2 19.9 %custom-call.111 = f32[2,128,128]{1,2,0:T(8,128)S(1)} custom-call(f32[2,128,128]{2,1,0:T(8,128)S(1)} %pad_maximum_fusion.40), custom_call_target="InvertDiagBlocksLowerTriangular" | custom-call | tf_op jit(solution)/shard_map/jit(_solve_triangular)/triangular_solve/custom-call.1 | solution.py:37
  476.0 11.7 %custom-call.112 = f32[1,128,128]{2,1,0:T(8,128)S(1)} custom-call(f32[1,128,128]{2,1,0:T(8,128)S(1)} %cholesky.1210), custom_call_target="Cholesky" | custom-call | tf_op jit(solution)/shard_map/jit(cholesky)/cholesky | solution.py:44
  506.6 20.1 %custom-call.115 = f32[2,128,128]{1,2,0:T(8,128)S(1)} custom-call(f32[2,128,128]{2,1,0:T(8,128)S(1)} %pad_maximum_fusion.41), custom_call_target="InvertDiagBlocksLowerTriangular" | custom-call | tf_op jit(solution)/shard_map/jit(_cho_solve)/triangular_solve | solution.py:45
  555.8 11.7 %custom-call.117 = f32[1,128,128]{2,1,0:T(8,128)S(1)} custom-call(f32[1,128,128]{2,1,0:T(8,128)S(1)} %copy.71), custom_call_target="Cholesky" | custom-call | tf_op jit(solution)/shard_map/jit(cholesky)/cholesky | solution.py:36
  586.7 19.9 %custom-call.120 = f32[2,128,128]{1,2,0:T(8,128)S(1)} custom-call(f32[2,128,128]{2,1,0:T(8,128)S(1)} %pad_maximum_fusion.42), custom_call_target="InvertDiagBlocksLowerTriangular" | custom-call | tf_op jit(solution)/shard_map/jit(_solve_triangular)/triangular_solve/custom-call.1 | solution.py:37
  609.5 11.7 %custom-call.121 = f32[1,128,128]{2,1,0:T(8,128)S(1)} custom-call(f32[1,128,128]{2,1,0:T(8,128)S(1)} %cholesky.1216), custom_call_target="Cholesky" | custom-call | tf_op jit(solution)/shard_map/jit(cholesky)/cholesky | solution.py:44
  640.1 20.1 %custom-call.124 = f32[2,128,128]{1,2,0:T(8,128)S(1)} custom-call(f32[2,128,128]{2,1,0:T(8,128)S(1)} %pad_maximum_fusion.43), custom_call_target="InvertDiagBlocksLowerTriangular" | custom-call | tf_op jit(solution)/shard_map/jit(_cho_solve)/triangular_solve | solution.py:45
  680.1 23.0 %collective-permute-done.10 = f32[2,1,192,384]{3,2,1,0:T(8,128)S(1)} collective-permute-done((f32[2,1,192,384]{3,2,1,0:T(8,128)S(1)}, f32[2,1,192,384]{3,2,1,0:T(8,128)S(1)}, u32[]{:S(2)}, u32[]{:S(2)}) %collective-permute-start.10) | collective-permute-done | bytes 589856 | tf_op jit(solution)/shard_map/ppermute | solution.py:10
  705.6 11.7 %custom-call.126 = f32[1,128,128]{2,1,0:T(8,128)S(1)} custom-call(f32[1,128,128]{2,1,0:T(8,128)S(1)} %copy.85), custom_call_target="Cholesky" | custom-call | tf_op jit(solution)/shard_map/jit(cholesky)/cholesky | solution.py:36
  736.5 19.9 %custom-call.129 = f32[2,128,128]{1,2,0:T(8,128)S(1)} custom-call(f32[2,128,128]{2,1,0:T(8,128)S(1)} %pad_maximum_fusion.44), custom_call_target="InvertDiagBlocksLowerTriangular" | custom-call | tf_op jit(solution)/shard_map/jit(_solve_triangular)/triangular_solve/custom-call.1 | solution.py:37
  759.3 11.7 %custom-call.130 = f32[1,128,128]{2,1,0:T(8,128)S(1)} custom-call(f32[1,128,128]{2,1,0:T(8,128)S(1)} %cholesky.1222), custom_call_target="Cholesky" | custom-call | tf_op jit(solution)/shard_map/jit(cholesky)/cholesky | solution.py:44
  789.9 20.1 %custom-call.133 = f32[2,128,128]{1,2,0:T(8,128)S(1)} custom-call(f32[2,128,128]{2,1,0:T(8,128)S(1)} %pad_maximum_fusion.45), custom_call_target="InvertDiagBlocksLowerTriangular" | custom-call | tf_op jit(solution)/shard_map/jit(_cho_solve)/triangular_solve | solution.py:45
  819.5 12.9 %collective-permute-start.11 = (f32[2,1,192,384]{3,2,1,0:T(8,128)S(1)}, f32[2,1,192,384]{3,2,1,0:T(8,128)S(1)}, u32[]{:S(2)}, u32[]{:S(2)}) collective-permute-start(f32[2,1,192,384]{3,2,1,0:T(8,128)S(1)} %pad_maximum_fusion.5), channel_id=1, source_target_pairs={{0,128},{4,132},{8,136},{12,140},{16,144},{20,148},{24,152},{28,15... | collective-permute-start | bytes 1769480 | tf_op jit(solution)/shard_map/ppermute | solution.py:10
  841.8 13.5 %collective-permute-done.11 = f32[2,1,192,384]{3,2,1,0:T(8,128)S(1)} collective-permute-done((f32[2,1,192,384]{3,2,1,0:T(8,128)S(1)}, f32[2,1,192,384]{3,2,1,0:T(8,128)S(1)}, u32[]{:S(2)}, u32[]{:S(2)}) %collective-permute-start.11) | collective-permute-done | bytes 589856 | tf_op jit(solution)/shard_map/ppermute | solution.py:10
  857.7 11.7 %custom-call.135 = f32[1,128,128]{2,1,0:T(8,128)S(1)} custom-call(f32[1,128,128]{2,1,0:T(8,128)S(1)} %cholesky.1225), custom_call_target="Cholesky" | custom-call | tf_op jit(solution)/shard_map/jit(cholesky)/cholesky | solution.py:36
  888.4 19.9 %custom-call.138 = f32[2,128,128]{1,2,0:T(8,128)S(1)} custom-call(f32[2,128,128]{2,1,0:T(8,128)S(1)} %pad_maximum_fusion.46), custom_call_target="InvertDiagBlocksLowerTriangular" | custom-call | tf_op jit(solution)/shard_map/jit(_solve_triangular)/triangular_solve/custom-call.1 | solution.py:37
  941.5 19.9 %custom-call.142 = f32[2,128,128]{1,2,0:T(8,128)S(1)} custom-call(f32[2,128,128]{2,1,0:T(8,128)S(1)} %pad_maximum_fusion.47), custom_call_target="InvertDiagBlocksLowerTriangular" | custom-call | tf_op jit(solution)/shard_map/jit(_cho_solve)/triangular_solve | solution.py:45
  966.8 30.9 %all-gather.3.cloned.1.call-done = f32[768,384]{1,0:T(8,128)} async-done(((f32[192,384]{1,0:T(8,128)}), f32[768,384]{1,0:T(8,128)}) %all-gather.3.cloned.1.call-update) | async-done | bytes 1179664 | tf_op jit(solution)/shard_map/all_gather | solution.py:108
  (561 shorter events, 450.8 us)
Async XLA Ops:
  7.2 990.5 %all-gather.3.cloned.1.call-start = ((), (), s32[]{:S(2)}) async-start(), calls=%async_computation | async-start | bytes 1474560 | tf_op jit(solution)/shard_map/all_gather | solution.py:108
  8.3 114.7 %collective-permute-start = (f32[192,192]{0,1:T(8,128)S(1)}, f32[192,192]{0,1:T(8,128)S(1)}, u32[]{:S(2)}, u32[]{:S(2)}) collective-permute-start(f32[192,192]{0,1:T(8,128)S(1)} %get-tuple-element.293), channel_id=1, source_target_pairs={{0,4},{4,8},{8,12},{12,16},{16,20},{20,24},{24,28},{28,32},{32,36}... | collective-permute-start | bytes 442376 | tf_op jit(solution)/shard_map/ppermute | solution.py:10
  124.1 11.0 %collective-permute-start.2 = (f32[2,1,192,384]{3,2,1,0:T(8,128)S(1)}, f32[2,1,192,384]{3,2,1,0:T(8,128)S(1)}, u32[]{:S(2)}, u32[]{:S(2)}) collective-permute-start(f32[2,1,192,384]{3,2,1,0:T(8,128)S(1)} %pad_maximum_fusion), channel_id=1, source_target_pairs={{4,0},{8,4},{12,8},{16,12},{20,16},{24,20},{28,24},{32,28},{36,32}... | collective-permute-start | bytes 1769480 | tf_op jit(solution)/shard_map/ppermute | solution.py:10
  127.7 11.2 %collective-permute-start.1 = (f32[2,1,192,384]{3,2,1,0:T(8,128)S(1)}, f32[2,1,192,384]{3,2,1,0:T(8,128)S(1)}, u32[]{:S(2)}, u32[]{:S(2)}) collective-permute-start(f32[2,1,192,384]{3,2,1,0:T(8,128)S(1)} %pad_maximum_fusion), channel_id=1, source_target_pairs={{0,4},{4,8},{8,12},{12,16},{16,20},{20,24},{24,28},{28,32},{32,36}... | collective-permute-start | bytes 1769480 | tf_op jit(solution)/shard_map/ppermute | solution.py:10
  254.1 16.3 %collective-permute-start.4 = (f32[2,1,192,384]{3,2,1,0:T(8,128)S(1)}, f32[2,1,192,384]{3,2,1,0:T(8,128)S(1)}, u32[]{:S(2)}, u32[]{:S(2)}) collective-permute-start(f32[2,1,192,384]{3,2,1,0:T(8,128)S(1)} %pad_maximum_fusion.1), channel_id=1, source_target_pairs={{8,0},{12,4},{16,8},{20,12},{24,16},{28,20},{32,24},{36,28},{40,32... | collective-permute-start | bytes 1769480 | tf_op jit(solution)/shard_map/ppermute | solution.py:10
  256.0 16.5 %collective-permute-start.3 = (f32[2,1,192,384]{3,2,1,0:T(8,128)S(1)}, f32[2,1,192,384]{3,2,1,0:T(8,128)S(1)}, u32[]{:S(2)}, u32[]{:S(2)}) collective-permute-start(f32[2,1,192,384]{3,2,1,0:T(8,128)S(1)} %pad_maximum_fusion.1), channel_id=1, source_target_pairs={{0,8},{4,12},{8,16},{12,20},{16,24},{20,28},{24,32},{28,36},{32,40... | collective-permute-start | bytes 1769480 | tf_op jit(solution)/shard_map/ppermute | solution.py:10
  387.5 19.6 %collective-permute-start.6 = (f32[2,1,192,384]{3,2,1,0:T(8,128)S(1)}, f32[2,1,192,384]{3,2,1,0:T(8,128)S(1)}, u32[]{:S(2)}, u32[]{:S(2)}) collective-permute-start(f32[2,1,192,384]{3,2,1,0:T(8,128)S(1)} %pad_maximum_fusion.2), channel_id=1, source_target_pairs={{16,0},{20,4},{24,8},{28,12},{32,16},{36,20},{40,24},{44,28},{48,3... | collective-permute-start | bytes 1769480 | tf_op jit(solution)/shard_map/ppermute | solution.py:10
  388.8 31.1 %collective-permute-start.5 = (f32[2,1,192,384]{3,2,1,0:T(8,128)S(1)}, f32[2,1,192,384]{3,2,1,0:T(8,128)S(1)}, u32[]{:S(2)}, u32[]{:S(2)}) collective-permute-start(f32[2,1,192,384]{3,2,1,0:T(8,128)S(1)} %pad_maximum_fusion.2), channel_id=1, source_target_pairs={{0,16},{4,20},{8,24},{12,28},{16,32},{20,36},{24,40},{28,44},{32,4... | collective-permute-start | bytes 1769480 | tf_op jit(solution)/shard_map/ppermute | solution.py:10
  534.9 17.3 %collective-permute-start.8 = (f32[2,1,192,384]{3,2,1,0:T(8,128)S(1)}, f32[2,1,192,384]{3,2,1,0:T(8,128)S(1)}, u32[]{:S(2)}, u32[]{:S(2)}) collective-permute-start(f32[2,1,192,384]{3,2,1,0:T(8,128)S(1)} %pad_maximum_fusion.3), channel_id=1, source_target_pairs={{32,0},{36,4},{40,8},{44,12},{48,16},{52,20},{56,24},{60,28},{64,3... | collective-permute-start | bytes 1769480 | tf_op jit(solution)/shard_map/ppermute | solution.py:10
  536.2 17.2 %collective-permute-start.7 = (f32[2,1,192,384]{3,2,1,0:T(8,128)S(1)}, f32[2,1,192,384]{3,2,1,0:T(8,128)S(1)}, u32[]{:S(2)}, u32[]{:S(2)}) collective-permute-start(f32[2,1,192,384]{3,2,1,0:T(8,128)S(1)} %pad_maximum_fusion.3), channel_id=1, source_target_pairs={{0,32},{4,36},{8,40},{12,44},{16,48},{20,52},{24,56},{28,60},{32,6... | collective-permute-start | bytes 1769480 | tf_op jit(solution)/shard_map/ppermute | solution.py:10
  668.4 34.6 %collective-permute-start.10 = (f32[2,1,192,384]{3,2,1,0:T(8,128)S(1)}, f32[2,1,192,384]{3,2,1,0:T(8,128)S(1)}, u32[]{:S(2)}, u32[]{:S(2)}) collective-permute-start(f32[2,1,192,384]{3,2,1,0:T(8,128)S(1)} %pad_maximum_fusion.4), channel_id=1, source_target_pairs={{64,0},{68,4},{72,8},{76,12},{80,16},{84,20},{88,24},{92,28},{96,3... | collective-permute-start | bytes 1769480 | tf_op jit(solution)/shard_map/ppermute | solution.py:10
  669.7 33.5 %collective-permute-start.9 = (f32[2,1,192,384]{3,2,1,0:T(8,128)S(1)}, f32[2,1,192,384]{3,2,1,0:T(8,128)S(1)}, u32[]{:S(2)}, u32[]{:S(2)}) collective-permute-start(f32[2,1,192,384]{3,2,1,0:T(8,128)S(1)} %pad_maximum_fusion.4), channel_id=1, source_target_pairs={{0,64},{4,68},{8,72},{12,76},{16,80},{20,84},{24,88},{28,92},{32,9... | collective-permute-start | bytes 1769480 | tf_op jit(solution)/shard_map/ppermute | solution.py:10
  818.2 23.4 %collective-permute-start.12 = (f32[2,1,192,384]{3,2,1,0:T(8,128)S(1)}, f32[2,1,192,384]{3,2,1,0:T(8,128)S(1)}, u32[]{:S(2)}, u32[]{:S(2)}) collective-permute-start(f32[2,1,192,384]{3,2,1,0:T(8,128)S(1)} %pad_maximum_fusion.5), channel_id=1, source_target_pairs={{128,0},{132,4},{136,8},{140,12},{144,16},{148,20},{152,24},{156,2... | collective-permute-start | bytes 1769480 | tf_op jit(solution)/shard_map/ppermute | solution.py:10
  819.5 35.7 %collective-permute-start.11 = (f32[2,1,192,384]{3,2,1,0:T(8,128)S(1)}, f32[2,1,192,384]{3,2,1,0:T(8,128)S(1)}, u32[]{:S(2)}, u32[]{:S(2)}) collective-permute-start(f32[2,1,192,384]{3,2,1,0:T(8,128)S(1)} %pad_maximum_fusion.5), channel_id=1, source_target_pairs={{0,128},{4,132},{8,136},{12,140},{16,144},{20,148},{24,152},{28,15... | collective-permute-start | bytes 1769480 | tf_op jit(solution)/shard_map/ppermute | solution.py:10
  964.2 2.5 copy-start.2
  997.7 3.5 copy-start
  1004.0 0.9 copy-start.1
Sparse Core Ops, SparseCore 0:
  966.8 30.8 all-gather.2
where the time goes:
time: 1020 us; the launch traced here: 1010 us
  other arithmetic  695 us (68%)
  waiting for transfers between devices  133 us (13%)
  matrix products  80.4 us (8%)
  starting transfers between devices  55.3 us (5%)
  between operations  37.5 us (4%)
  local copies, waits for them, and re-layouts  12.5 us (1%)
    another operation x49, other arithmetic, invert(): imag_factor = jnp.linalg.cholesky(imag_part)  201 us
    another operation x49, other arithmetic, invert(): square_factor = jnp.linalg.cholesky(squared)  201 us
    another operation x28, other arithmetic, invert(): jax.scipy.linalg.cho_solve((square_factor, True), factor_inverse)  141 us
    another operation x30, other arithmetic, invert(): jax.scipy.linalg.solve_triangular(imag_factor, identity, lower=True)  140 us
    ppermute x13, waiting for transfers between devices, shifted(): lax.ppermute(value, axis, [(source, source + steps) for source in range(f...  102 us
    ppermute x13, starting transfers between devices, shifted(): lax.ppermute(value, axis, [(source, source + steps) for source in range(f...  55.2 us
    dot_general x48, matrix products, complex_product(): return jnp.einsum('...ij,...jk->...ik', left, stacked, precision=high)  39.3 us
    all_gather x1, waiting for transfers between devices, shards(): lax.all_gather(green_local[:, None], 'energy', axis=0, tiled=True)[:, 0]  30.9 us
  transfers between devices with their start and end apart: 14, of which 12 were waited for; matrix products, arithmetic and copies ran while one was open for 11% of the time, Pallas kernels for 0%

commit v1 on v0

--- a/solution.py
+++ b/solution.py
@@ -1,7 +1,34 @@
+import functools
 import jax
 import jax.numpy as jnp
 from jax import lax
 from jax.sharding import PartitionSpec as P
+
+
+def files_derive(q_in, axis_name):
+    outer = lax.psum(1, axis_name)
+    all_values = lax.axis_index(axis_name)
+    y, k_now, z2 = (outer, all_values, q_in.shape[0])
+    history = []
+    for dev in range(y):
+        history.append((dev, (dev + 1) % y))
+    inbox = []
+    for dev in range(y):
+        inbox.append((dev, (dev - 1) % y))
+    shaped = jnp.zeros((*q_in.shape[:0], y * z2, *q_in.shape[1:]), q_in.dtype)
+    shaped = lax.dynamic_update_slice_in_dim(shaped, q_in, k_now * z2, axis=0)
+    long_array = y1 = q_in
+    e_next = y // 2
+    for ii in range(1, e_next + 1):
+        long_array = lax.ppermute(long_array, axis_name, history)
+        shaped = lax.dynamic_update_slice_in_dim(shaped, long_array, (k_now - ii) % y * z2, axis=0)
+        if ii < y - e_next:
+            y1 = lax.ppermute(y1, axis_name, inbox)
+            shaped = lax.dynamic_update_slice_in_dim(shaped, y1, (k_now + ii) % y * z2, axis=0)
+    return shaped
+
+
+measure_case = functools.partial(files_derive, axis_name="energy")
 
 
 def shifted(value, axis, steps):
@@ -105,7 +132,7 @@
     upper_all = jnp.broadcast_to(upper_one, (energy_count, block_width, 2 * block_width))
     lower_all = jnp.broadcast_to(lower_one, (energy_count, block_width, 2 * block_width))
     green_local = reduce_levels(matrix, lower_all, upper_all)
-    everyone = lax.all_gather(green_local[:, None], "energy", axis=0, tiled=True)[:, 0]
+    everyone = measure_case(green_local[:, None])[:, 0]
     pair_count = energy_pairs.shape[1]
     first = jnp.take(everyone, energy_pairs[:, :, 0], axis=0)
     second = jnp.take(everyone, energy_pairs[:, :, 1], axis=0)

time: 1020 us -> 993 us (0.974)
  waiting for transfers between devices: 133 us -> 114 us
  between operations: 37.5 us -> 24.2 us
    all_gather x1 -> x0, waiting for transfers between devices: 30.9 us -> none  [shards(): lax.all_gather(green_local[:, None], 'energy', axis=0, tiled=True)[:, 0]]
    ppermute x0 -> x3, waiting for transfers between devices: none -> 12.2 us  [the longest x2 12.2 us: files_derive(): long_array = lax.ppermute(long_array, axis_name, history)]
  transfers between devices with their start and end apart: 14 -> 16, of which waited for: 12 -> 13; matrix products, arithmetic and copies ran while one was open for 11% -> 11% of each run, Pallas kernels for 0% -> 0%
where the time goes in v1:
time: 993 us; the launch traced here: 983 us
  other arithmetic  695 us (70%)
  waiting for transfers between devices  114 us (11%)
  matrix products  79.7 us (8%)
  starting transfers between devices  58.9 us (6%)
  between operations  24.2 us (2%)
  local copies, waits for them, and re-layouts  11.3 us (1%)
    another operation x49, other arithmetic, invert(): imag_factor = jnp.linalg.cholesky(imag_part)  201 us
    another operation x49, other arithmetic, invert(): square_factor = jnp.linalg.cholesky(squared)  201 us
    another operation x28, other arithmetic, invert(): jax.scipy.linalg.cho_solve((square_factor, True), factor_inverse)  141 us
    another operation x30, other arithmetic, invert(): jax.scipy.linalg.solve_triangular(imag_factor, identity, lower=True)  140 us
    ppermute x13, waiting for transfers between devices, shifted(): lax.ppermute(value, axis, [(source, source + steps) for source in range(f...  102 us
    ppermute x13, starting transfers between devices, shifted(): lax.ppermute(value, axis, [(source, source + steps) for source in range(f...  55.3 us
    dot_general x48, matrix products, complex_product(): return jnp.einsum('...ij,...jk->...ik', left, stacked, precision=high)  38.6 us
  transfers between devices with their start and end apart: 16, of which 13 were waited for; matrix products, arithmetic and copies ran while one was open for 11% of the time, Pallas kernels for 0%

profile of v1, /device:TPU:2, one launch (start us, length us, event | category | flops | bytes accessed | tf_op | source)
XLA Modules:
  0.0 982.7 jit_solution(16893173767106023227)
XLA Ops:
  6.8 11.7 %custom-call.81 = f32[1,128,128]{2,1,0:T(8,128)S(1)} custom-call(f32[1,128,128]{2,1,0:T(8,128)S(1)} %copy.15), custom_call_target="Cholesky" | custom-call | tf_op jit(solution)/shard_map/jit(cholesky)/cholesky | solution.py:63
  37.5 19.9 %custom-call.84 = f32[2,128,128]{1,2,0:T(8,128)S(1)} custom-call(f32[2,128,128]{2,1,0:T(8,128)S(1)} %pad_maximum_fusion.34), custom_call_target="InvertDiagBlocksLowerTriangular" | custom-call | tf_op jit(solution)/shard_map/jit(_solve_triangular)/triangular_solve/custom-call.1 | solution.py:64
  60.3 11.7 %custom-call.85 = f32[1,128,128]{2,1,0:T(8,128)S(1)} custom-call(f32[1,128,128]{2,1,0:T(8,128)S(1)} %cholesky.1192), custom_call_target="Cholesky" | custom-call | tf_op jit(solution)/shard_map/jit(cholesky)/cholesky | solution.py:71
  90.9 20.1 %custom-call.88 = f32[2,128,128]{1,2,0:T(8,128)S(1)} custom-call(f32[2,128,128]{2,1,0:T(8,128)S(1)} %pad_maximum_fusion.35), custom_call_target="InvertDiagBlocksLowerTriangular" | custom-call | tf_op jit(solution)/shard_map/jit(_cho_solve)/triangular_solve | solution.py:72
  134.8 11.7 %custom-call.90 = f32[1,128,128]{2,1,0:T(8,128)S(1)} custom-call(f32[1,128,128]{2,1,0:T(8,128)S(1)} %copy.29), custom_call_target="Cholesky" | custom-call | tf_op jit(solution)/shard_map/jit(cholesky)/cholesky | solution.py:63
  165.7 19.9 %custom-call.93 = f32[2,128,128]{1,2,0:T(8,128)S(1)} custom-call(f32[2,128,128]{2,1,0:T(8,128)S(1)} %pad_maximum_fusion.36), custom_call_target="InvertDiagBlocksLowerTriangular" | custom-call | tf_op jit(solution)/shard_map/jit(_solve_triangular)/triangular_solve/custom-call.1 | solution.py:64
  188.5 11.7 %custom-call.94 = f32[1,128,128]{2,1,0:T(8,128)S(1)} custom-call(f32[1,128,128]{2,1,0:T(8,128)S(1)} %cholesky.1198), custom_call_target="Cholesky" | custom-call | tf_op jit(solution)/shard_map/jit(cholesky)/cholesky | solution.py:71
  219.1 20.1 %custom-call.97 = f32[2,128,128]{1,2,0:T(8,128)S(1)} custom-call(f32[2,128,128]{2,1,0:T(8,128)S(1)} %pad_maximum_fusion.37), custom_call_target="InvertDiagBlocksLowerTriangular" | custom-call | tf_op jit(solution)/shard_map/jit(_cho_solve)/triangular_solve | solution.py:72
  268.3 11.7 %custom-call.99 = f32[1,128,128]{2,1,0:T(8,128)S(1)} custom-call(f32[1,128,128]{2,1,0:T(8,128)S(1)} %copy.43), custom_call_target="Cholesky" | custom-call | tf_op jit(solution)/shard_map/jit(cholesky)/cholesky | solution.py:63
  299.2 19.9 %custom-call.102 = f32[2,128,128]{1,2,0:T(8,128)S(1)} custom-call(f32[2,128,128]{2,1,0:T(8,128)S(1)} %pad_maximum_fusion.38), custom_call_target="InvertDiagBlocksLowerTriangular" | custom-call | tf_op jit(solution)/shard_map/jit(_solve_triangular)/triangular_solve/custom-call.1 | solution.py:64
  322.0 11.7 %custom-call.103 = f32[1,128,128]{2,1,0:T(8,128)S(1)} custom-call(f32[1,128,128]{2,1,0:T(8,128)S(1)} %cholesky.1204), custom_call_target="Cholesky" | custom-call | tf_op jit(solution)/shard_map/jit(cholesky)/cholesky | solution.py:71
  352.6 20.1 %custom-call.106 = f32[2,128,128]{1,2,0:T(8,128)S(1)} custom-call(f32[2,128,128]{2,1,0:T(8,128)S(1)} %pad_maximum_fusion.39), custom_call_target="InvertDiagBlocksLowerTriangular" | custom-call | tf_op jit(solution)/shard_map/jit(_cho_solve)/triangular_solve | solution.py:72
  400.7 12.6 %collective-permute-done.5 = f32[2,1,192,384]{3,2,1,0:T(8,128)S(1)} collective-permute-done((f32[2,1,192,384]{3,2,1,0:T(8,128)S(1)}, f32[2,1,192,384]{3,2,1,0:T(8,128)S(1)}, u32[]{:S(2)}, u32[]{:S(2)}) %collective-permute-start.5) | collective-permute-done | bytes 589856 | tf_op jit(solution)/shard_map/ppermute | solution.py:37
  415.8 11.7 %custom-call.108 = f32[1,128,128]{2,1,0:T(8,128)S(1)} custom-call(f32[1,128,128]{2,1,0:T(8,128)S(1)} %copy.57), custom_call_target="Cholesky" | custom-call | tf_op jit(solution)/shard_map/jit(cholesky)/cholesky | solution.py:63
  446.6 19.9 %custom-call.111 = f32[2,128,128]{1,2,0:T(8,128)S(1)} custom-call(f32[2,128,128]{2,1,0:T(8,128)S(1)} %pad_maximum_fusion.40), custom_call_target="InvertDiagBlocksLowerTriangular" | custom-call | tf_op jit(solution)/shard_map/jit(_solve_triangular)/triangular_solve/custom-call.1 | solution.py:64
  469.4 11.7 %custom-call.112 = f32[1,128,128]{2,1,0:T(8,128)S(1)} custom-call(f32[1,128,128]{2,1,0:T(8,128)S(1)} %cholesky.1210), custom_call_target="Cholesky" | custom-call | tf_op jit(solution)/shard_map/jit(cholesky)/cholesky | solution.py:71
  500.0 20.1 %custom-call.115 = f32[2,128,128]{1,2,0:T(8,128)S(1)} custom-call(f32[2,128,128]{2,1,0:T(8,128)S(1)} %pad_maximum_fusion.41), custom_call_target="InvertDiagBlocksLowerTriangular" | custom-call | tf_op jit(solution)/shard_map/jit(_cho_solve)/triangular_solve | solution.py:72
  549.3 11.7 %custom-call.117 = f32[1,128,128]{2,1,0:T(8,128)S(1)} custom-call(f32[1,128,128]{2,1,0:T(8,128)S(1)} %copy.71), custom_call_target="Cholesky" | custom-call | tf_op jit(solution)/shard_map/jit(cholesky)/cholesky | solution.py:63
  580.1 19.9 %custom-call.120 = f32[2,128,128]{1,2,0:T(8,128)S(1)} custom-call(f32[2,128,128]{2,1,0:T(8,128)S(1)} %pad_maximum_fusion.42), custom_call_target="InvertDiagBlocksLowerTriangular" | custom-call | tf_op jit(solution)/shard_map/jit(_solve_triangular)/triangular_solve/custom-call.1 | solution.py:64
  602.9 11.7 %custom-call.121 = f32[1,128,128]{2,1,0:T(8,128)S(1)} custom-call(f32[1,128,128]{2,1,0:T(8,128)S(1)} %cholesky.1216), custom_call_target="Cholesky" | custom-call | tf_op jit(solution)/shard_map/jit(cholesky)/cholesky | solution.py:71
  633.5 20.1 %custom-call.124 = f32[2,128,128]{1,2,0:T(8,128)S(1)} custom-call(f32[2,128,128]{2,1,0:T(8,128)S(1)} %pad_maximum_fusion.43), custom_call_target="InvertDiagBlocksLowerTriangular" | custom-call | tf_op jit(solution)/shard_map/jit(_cho_solve)/triangular_solve | solution.py:72
  673.5 23.0 %collective-permute-done.10 = f32[2,1,192,384]{3,2,1,0:T(8,128)S(1)} collective-permute-done((f32[2,1,192,384]{3,2,1,0:T(8,128)S(1)}, f32[2,1,192,384]{3,2,1,0:T(8,128)S(1)}, u32[]{:S(2)}, u32[]{:S(2)}) %collective-permute-start.10) | collective-permute-done | bytes 589856 | tf_op jit(solution)/shard_map/ppermute | solution.py:37
  699.1 11.7 %custom-call.126 = f32[1,128,128]{2,1,0:T(8,128)S(1)} custom-call(f32[1,128,128]{2,1,0:T(8,128)S(1)} %copy.85), custom_call_target="Cholesky" | custom-call | tf_op jit(solution)/shard_map/jit(cholesky)/cholesky | solution.py:63
  729.9 19.9 %custom-call.129 = f32[2,128,128]{1,2,0:T(8,128)S(1)} custom-call(f32[2,128,128]{2,1,0:T(8,128)S(1)} %pad_maximum_fusion.44), custom_call_target="InvertDiagBlocksLowerTriangular" | custom-call | tf_op jit(solution)/shard_map/jit(_solve_triangular)/triangular_solve/custom-call.1 | solution.py:64
  752.7 11.7 %custom-call.130 = f32[1,128,128]{2,1,0:T(8,128)S(1)} custom-call(f32[1,128,128]{2,1,0:T(8,128)S(1)} %cholesky.1222), custom_call_target="Cholesky" | custom-call | tf_op jit(solution)/shard_map/jit(cholesky)/cholesky | solution.py:71
  783.3 20.1 %custom-call.133 = f32[2,128,128]{1,2,0:T(8,128)S(1)} custom-call(f32[2,128,128]{2,1,0:T(8,128)S(1)} %pad_maximum_fusion.45), custom_call_target="InvertDiagBlocksLowerTriangular" | custom-call | tf_op jit(solution)/shard_map/jit(_cho_solve)/triangular_solve | solution.py:72
  813.0 12.9 %collective-permute-start.11 = (f32[2,1,192,384]{3,2,1,0:T(8,128)S(1)}, f32[2,1,192,384]{3,2,1,0:T(8,128)S(1)}, u32[]{:S(2)}, u32[]{:S(2)}) collective-permute-start(f32[2,1,192,384]{3,2,1,0:T(8,128)S(1)} %pad_maximum_fusion.5), channel_id=1, source_target_pairs={{0,128},{4,132},{8,136},{12,140},{16,144},{20,148},{24,152},{28,15... | collective-permute-start | bytes 1769480 | tf_op jit(solution)/shard_map/ppermute | solution.py:37
  835.3 13.5 %collective-permute-done.11 = f32[2,1,192,384]{3,2,1,0:T(8,128)S(1)} collective-permute-done((f32[2,1,192,384]{3,2,1,0:T(8,128)S(1)}, f32[2,1,192,384]{3,2,1,0:T(8,128)S(1)}, u32[]{:S(2)}, u32[]{:S(2)}) %collective-permute-start.11) | collective-permute-done | bytes 589856 | tf_op jit(solution)/shard_map/ppermute | solution.py:37
  851.1 11.7 %custom-call.135 = f32[1,128,128]{2,1,0:T(8,128)S(1)} custom-call(f32[1,128,128]{2,1,0:T(8,128)S(1)} %cholesky.1225), custom_call_target="Cholesky" | custom-call | tf_op jit(solution)/shard_map/jit(cholesky)/cholesky | solution.py:63
  881.9 19.9 %custom-call.138 = f32[2,128,128]{1,2,0:T(8,128)S(1)} custom-call(f32[2,128,128]{2,1,0:T(8,128)S(1)} %pad_maximum_fusion.46), custom_call_target="InvertDiagBlocksLowerTriangular" | custom-call | tf_op jit(solution)/shard_map/jit(_solve_triangular)/triangular_solve/custom-call.1 | solution.py:64
  904.4 11.7 %custom-call.139 = f32[1,128,128]{2,1,0:T(8,128)S(1)} custom-call(f32[1,128,128]{2,1,0:T(8,128)S(1)} %cholesky.1228), custom_call_target="Cholesky" | custom-call | tf_op jit(solution)/shard_map/jit(cholesky)/cholesky | solution.py:71
  935.0 19.9 %custom-call.142 = f32[2,128,128]{1,2,0:T(8,128)S(1)} custom-call(f32[2,128,128]{2,1,0:T(8,128)S(1)} %pad_maximum_fusion.47), custom_call_target="InvertDiagBlocksLowerTriangular" | custom-call | tf_op jit(solution)/shard_map/jit(_cho_solve)/triangular_solve | solution.py:72
  (568 shorter events, 453.0 us)
Async XLA Ops:
  1.7 114.7 %collective-permute-start = (f32[192,192]{0,1:T(8,128)S(1)}, f32[192,192]{0,1:T(8,128)S(1)}, u32[]{:S(2)}, u32[]{:S(2)}) collective-permute-start(f32[192,192]{0,1:T(8,128)S(1)} %get-tuple-element.293), channel_id=1, source_target_pairs={{0,4},{4,8},{8,12},{12,16},{16,20},{20,24},{24,28},{28,32},{32,36}... | collective-permute-start | bytes 442376 | tf_op jit(solution)/shard_map/ppermute | solution.py:37
  117.5 11.0 %collective-permute-start.2 = (f32[2,1,192,384]{3,2,1,0:T(8,128)S(1)}, f32[2,1,192,384]{3,2,1,0:T(8,128)S(1)}, u32[]{:S(2)}, u32[]{:S(2)}) collective-permute-start(f32[2,1,192,384]{3,2,1,0:T(8,128)S(1)} %pad_maximum_fusion), channel_id=1, source_target_pairs={{4,0},{8,4},{12,8},{16,12},{20,16},{24,20},{28,24},{32,28},{36,32}... | collective-permute-start | bytes 1769480 | tf_op jit(solution)/shard_map/ppermute | solution.py:37
  121.1 11.2 %collective-permute-start.1 = (f32[2,1,192,384]{3,2,1,0:T(8,128)S(1)}, f32[2,1,192,384]{3,2,1,0:T(8,128)S(1)}, u32[]{:S(2)}, u32[]{:S(2)}) collective-permute-start(f32[2,1,192,384]{3,2,1,0:T(8,128)S(1)} %pad_maximum_fusion), channel_id=1, source_target_pairs={{0,4},{4,8},{8,12},{12,16},{16,20},{20,24},{24,28},{28,32},{32,36}... | collective-permute-start | bytes 1769480 | tf_op jit(solution)/shard_map/ppermute | solution.py:37
  247.5 16.3 %collective-permute-start.4 = (f32[2,1,192,384]{3,2,1,0:T(8,128)S(1)}, f32[2,1,192,384]{3,2,1,0:T(8,128)S(1)}, u32[]{:S(2)}, u32[]{:S(2)}) collective-permute-start(f32[2,1,192,384]{3,2,1,0:T(8,128)S(1)} %pad_maximum_fusion.1), channel_id=1, source_target_pairs={{8,0},{12,4},{16,8},{20,12},{24,16},{28,20},{32,24},{36,28},{40,32... | collective-permute-start | bytes 1769480 | tf_op jit(solution)/shard_map/ppermute | solution.py:37
  249.4 16.5 %collective-permute-start.3 = (f32[2,1,192,384]{3,2,1,0:T(8,128)S(1)}, f32[2,1,192,384]{3,2,1,0:T(8,128)S(1)}, u32[]{:S(2)}, u32[]{:S(2)}) collective-permute-start(f32[2,1,192,384]{3,2,1,0:T(8,128)S(1)} %pad_maximum_fusion.1), channel_id=1, source_target_pairs={{0,8},{4,12},{8,16},{12,20},{16,24},{20,28},{24,32},{28,36},{32,40... | collective-permute-start | bytes 1769480 | tf_op jit(solution)/shard_map/ppermute | solution.py:37
  380.9 19.6 %collective-permute-start.6 = (f32[2,1,192,384]{3,2,1,0:T(8,128)S(1)}, f32[2,1,192,384]{3,2,1,0:T(8,128)S(1)}, u32[]{:S(2)}, u32[]{:S(2)}) collective-permute-start(f32[2,1,192,384]{3,2,1,0:T(8,128)S(1)} %pad_maximum_fusion.2), channel_id=1, source_target_pairs={{16,0},{20,4},{24,8},{28,12},{32,16},{36,20},{40,24},{44,28},{48,3... | collective-permute-start | bytes 1769480 | tf_op jit(solution)/shard_map/ppermute | solution.py:37
  382.2 31.1 %collective-permute-start.5 = (f32[2,1,192,384]{3,2,1,0:T(8,128)S(1)}, f32[2,1,192,384]{3,2,1,0:T(8,128)S(1)}, u32[]{:S(2)}, u32[]{:S(2)}) collective-permute-start(f32[2,1,192,384]{3,2,1,0:T(8,128)S(1)} %pad_maximum_fusion.2), channel_id=1, source_target_pairs={{0,16},{4,20},{8,24},{12,28},{16,32},{20,36},{24,40},{28,44},{32,4... | collective-permute-start | bytes 1769480 | tf_op jit(solution)/shard_map/ppermute | solution.py:37
  528.4 17.3 %collective-permute-start.8 = (f32[2,1,192,384]{3,2,1,0:T(8,128)S(1)}, f32[2,1,192,384]{3,2,1,0:T(8,128)S(1)}, u32[]{:S(2)}, u32[]{:S(2)}) collective-permute-start(f32[2,1,192,384]{3,2,1,0:T(8,128)S(1)} %pad_maximum_fusion.3), channel_id=1, source_target_pairs={{32,0},{36,4},{40,8},{44,12},{48,16},{52,20},{56,24},{60,28},{64,3... | collective-permute-start | bytes 1769480 | tf_op jit(solution)/shard_map/ppermute | solution.py:37
  529.7 17.2 %collective-permute-start.7 = (f32[2,1,192,384]{3,2,1,0:T(8,128)S(1)}, f32[2,1,192,384]{3,2,1,0:T(8,128)S(1)}, u32[]{:S(2)}, u32[]{:S(2)}) collective-permute-start(f32[2,1,192,384]{3,2,1,0:T(8,128)S(1)} %pad_maximum_fusion.3), channel_id=1, source_target_pairs={{0,32},{4,36},{8,40},{12,44},{16,48},{20,52},{24,56},{28,60},{32,6... | collective-permute-start | bytes 1769480 | tf_op jit(solution)/shard_map/ppermute | solution.py:37
  661.8 34.6 %collective-permute-start.10 = (f32[2,1,192,384]{3,2,1,0:T(8,128)S(1)}, f32[2,1,192,384]{3,2,1,0:T(8,128)S(1)}, u32[]{:S(2)}, u32[]{:S(2)}) collective-permute-start(f32[2,1,192,384]{3,2,1,0:T(8,128)S(1)} %pad_maximum_fusion.4), channel_id=1, source_target_pairs={{64,0},{68,4},{72,8},{76,12},{80,16},{84,20},{88,24},{92,28},{96,3... | collective-permute-start | bytes 1769480 | tf_op jit(solution)/shard_map/ppermute | solution.py:37
  663.1 33.5 %collective-permute-start.9 = (f32[2,1,192,384]{3,2,1,0:T(8,128)S(1)}, f32[2,1,192,384]{3,2,1,0:T(8,128)S(1)}, u32[]{:S(2)}, u32[]{:S(2)}) collective-permute-start(f32[2,1,192,384]{3,2,1,0:T(8,128)S(1)} %pad_maximum_fusion.4), channel_id=1, source_target_pairs={{0,64},{4,68},{8,72},{12,76},{16,80},{20,84},{24,88},{28,92},{32,9... | collective-permute-start | bytes 1769480 | tf_op jit(solution)/shard_map/ppermute | solution.py:37
  810.0 15.9 %copy-start.2 = (s32[1,8,2]{1,2,0:T(2,128)S(1)}, s32[1,8,2]{1,2,0:T(2,128)}, u32[]{:S(2)}) copy-start(s32[1,8,2]{1,2,0:T(2,128)} %param.20) | copy-start | bytes 196
  811.7 23.4 %collective-permute-start.12 = (f32[2,1,192,384]{3,2,1,0:T(8,128)S(1)}, f32[2,1,192,384]{3,2,1,0:T(8,128)S(1)}, u32[]{:S(2)}, u32[]{:S(2)}) collective-permute-start(f32[2,1,192,384]{3,2,1,0:T(8,128)S(1)} %pad_maximum_fusion.5), channel_id=1, source_target_pairs={{128,0},{132,4},{136,8},{140,12},{144,16},{148,20},{152,24},{156,2... | collective-permute-start | bytes 1769480 | tf_op jit(solution)/shard_map/ppermute | solution.py:37
  813.0 35.7 %collective-permute-start.11 = (f32[2,1,192,384]{3,2,1,0:T(8,128)S(1)}, f32[2,1,192,384]{3,2,1,0:T(8,128)S(1)}, u32[]{:S(2)}, u32[]{:S(2)}) collective-permute-start(f32[2,1,192,384]{3,2,1,0:T(8,128)S(1)} %pad_maximum_fusion.5), channel_id=1, source_target_pairs={{0,128},{4,132},{8,136},{12,140},{16,144},{20,148},{24,152},{28,15... | collective-permute-start | bytes 1769480 | tf_op jit(solution)/shard_map/ppermute | solution.py:37
  959.5 18.1 %copy-start = (f32[192,384]{1,0:T(8,128)}, f32[192,384]{1,0:T(8,128)S(1)}, u32[]{:S(2)}) copy-start(f32[192,384]{1,0:T(8,128)S(1)} %get-tuple-element.385) | copy-start | bytes 884740
  959.5 8.0 collective-permute-start.13
  961.2 6.7 collective-permute-start.14
  967.5 7.9 collective-permute-start.15
  980.4 0.9 copy-start.1
